TPU v7x, 256 devices: a whole 4x4x8 slice. The times are simulated.
256 devices in a mesh: gx: 4 (over x), gy: 8 (over y, core), gz: 8 (over z).
Axes of the slice: x: 4, y: 4, z: 8, core: 2. Of those that a mesh axis runs over, the one named last changes fastest.
Arguments:
- orbitals: bfloat16 [32, 64, 128, 256], P('gx', 'gy', 'gz'), may hold values from -120 to 120
- cell_block: bfloat16 [729, 729], replicated, may hold values from -0.4 to 2.4, as said below
- potential: float32 [32, 64, 128], P('gx', 'gy', 'gz'), may hold values from -1 to 1
Outputs:
- orthonormal: bfloat16 [32, 64, 128, 256], P('gx', 'gy', 'gz')
Inputs may be any that keep to these rules, and one draw needn't show every extreme that they name: `cell_block`: symmetric.
All inputs are finite; a program needn't handle non-finite values.
Results may differ from a plain program's by a relative error of at most 0.01.
Values may be sent and summed in bfloat16 or wider, within the bound.
A program may use at most 64 MiB of HBM per device.

v0:
```python
import jax
import jax.numpy as jnp
from jax import lax
from jax.sharding import PartitionSpec as P

POLY = 8


CENTER = 6.0
HALF_WIDTH = 8.0


def passed_along(block, axis, distance):
    devices = range(lax.axis_size(axis))
    route = [((i - distance) % len(devices), i) for i in devices]
    return lax.ppermute(block, axis, route)


def windows(values, which_axis, cell_count):
    span = POLY * cell_count
    leading = lax.slice_in_dim(values, 0, span, axis=which_axis)
    dims_now = leading.shape
    leading = leading.reshape(
        dims_now[:which_axis] + (cell_count, POLY) + dims_now[which_axis + 1 :]
    )
    end_nodes = lax.slice_in_dim(values, POLY, span + 1, stride=POLY, axis=which_axis)
    end_nodes = jnp.expand_dims(end_nodes, which_axis + 1)
    return jnp.concatenate([leading, end_nodes], axis=which_axis + 1)


def fold(pieces, which_axis):
    cell_count = pieces.shape[which_axis]
    first_node = lax.slice_in_dim(pieces, 0, 1, axis=which_axis + 1)
    inner_nodes = lax.slice_in_dim(pieces, 1, POLY, axis=which_axis + 1)
    last_node = lax.slice_in_dim(pieces, POLY, POLY + 1, axis=which_axis + 1)
    earlier = lax.slice_in_dim(last_node, 0, cell_count - 1, axis=which_axis)
    blank = jnp.zeros_like(lax.slice_in_dim(last_node, 0, 1, axis=which_axis))
    first_node = first_node + jnp.concatenate([blank, earlier], axis=which_axis)
    merged = jnp.concatenate([first_node, inner_nodes], axis=which_axis + 1)
    dims_now = merged.shape
    merged = merged.reshape(
        dims_now[:which_axis] + (cell_count * POLY,) + dims_now[which_axis + 2 :]
    )
    closing = lax.slice_in_dim(last_node, cell_count - 1, cell_count, axis=which_axis)
    closing = jnp.squeeze(closing, which_axis + 1)
    return jnp.concatenate([merged, closing], axis=which_axis)


def cell_product(extended, cell_block):
    side = POLY + 1
    count_x = (extended.shape[0] - 1) // POLY
    count_y = (extended.shape[1] - 1) // POLY
    count_z = (extended.shape[2] - 1) // POLY
    pieces = windows(extended, 0, count_x)
    pieces = windows(pieces, 2, count_y)
    pieces = windows(pieces, 4, count_z)
    width = pieces.shape[-1]
    cells = pieces.transpose(0, 2, 4, 1, 3, 5, 6).reshape(
        count_x * count_y * count_z, side**3, width
    )
    product = jnp.einsum("ij,cjo->cio", cell_block, cells, preferred_element_type=jnp.float32)
    product = product.reshape(count_x, count_y, count_z, side, side, side, width).transpose(
        0, 3, 1, 4, 2, 5, 6
    )
    return fold(fold(fold(product, 4), 2), 0)


def fetch(values, which_axis):
    face_layer = lax.slice_in_dim(values, 0, 1, axis=which_axis)
    if which_axis == 0:
        received = passed_along(face_layer, "gx", -1)
    elif which_axis == 1:
        received = passed_along(face_layer, "gy", -1)
    else:
        received = passed_along(face_layer, "gz", -1)
    return jnp.concatenate([values, received], axis=which_axis)


def fetch_all(values):
    extended = values
    for which_axis in (2, 1, 0):
        extended = fetch(extended, which_axis)
    return extended


def settle(assembled, which_axis):
    inner_size = assembled.shape[which_axis] - 1
    face_layer = lax.slice_in_dim(assembled, inner_size, inner_size + 1, axis=which_axis)
    if which_axis == 0:
        received = passed_along(face_layer.astype(jnp.bfloat16), "gx", 1).astype(face_layer.dtype)
    elif which_axis == 1:
        received = passed_along(face_layer, "gy", 1)
    else:
        received = passed_along(face_layer, "gz", 1)
    leading = lax.slice_in_dim(assembled, 0, 1, axis=which_axis) + received
    remaining = lax.slice_in_dim(assembled, 1, inner_size, axis=which_axis)
    return jnp.concatenate([leading, remaining], axis=which_axis)


def chebyshev(apply_step, orbitals):
    start_values = orbitals.astype(jnp.float32)
    image = apply_step(orbitals)
    first = ((image - CENTER * start_values) / HALF_WIDTH).astype(jnp.bfloat16)
    image = apply_step(first)
    second = (
        2.0 * (image - CENTER * first.astype(jnp.float32)) / HALF_WIDTH - start_values
    ).astype(jnp.bfloat16)
    image = apply_step(second)
    return (
        2.0 * (image - CENTER * second.astype(jnp.float32)) / HALF_WIDTH - first.astype(jnp.float32)
    ).astype(jnp.bfloat16)


def local(orbitals, cell_block, potential):

    def apply_operator(values):
        assembled = cell_product(fetch_all(values), cell_block)
        for which_axis in (0, 1, 2):
            assembled = settle(assembled, which_axis)
        return assembled + potential[..., None] * values.astype(jnp.float32)

    filtered = chebyshev(apply_operator, orbitals)
    width = filtered.shape[-1]
    flat_rows = filtered.reshape(-1, width)
    node_total = (
        flat_rows.shape[0] * lax.axis_size("gx") * lax.axis_size("gy") * lax.axis_size("gz")
    )
    local_gram = lax.dot_general(
        flat_rows, flat_rows, (((0,), (0,)), ((), ())), preferred_element_type=jnp.float32
    )
    gram = lax.psum(local_gram, ("gx", "gy", "gz"))
    lower = jnp.linalg.cholesky(gram / node_total)
    inverse = jax.scipy.linalg.solve_triangular(
        lower, jnp.eye(width, dtype=jnp.float32), lower=True
    )
    right_factor = inverse.T
    factor_high = right_factor.astype(jnp.bfloat16)
    factor_low = (right_factor - factor_high.astype(jnp.float32)).astype(jnp.bfloat16)
    rotated = jnp.dot(flat_rows, factor_high, preferred_element_type=jnp.float32) + jnp.dot(
        flat_rows, factor_low, preferred_element_type=jnp.float32
    )
    return rotated.astype(jnp.bfloat16).reshape(filtered.shape)


def solution(mesh):
    placed = (P("gx", "gy", "gz", None), P(), P("gx", "gy", "gz"))
    return jax.shard_map(
        local, mesh=mesh, in_specs=placed, out_specs=P("gx", "gy", "gz", None), check_vma=False
    )
```

profile of v0, /device:TPU:2, one launch (start us, length us, event | category | flops | bytes accessed | tf_op | source)
XLA Modules:
  0.0 453.2 jit_solution(10956627082531560603)
XLA Ops:
  7.6 5.9 %collective-permute-start = (bf16[8,8,1,256]{3,2,1,0:T(2,128)(2,1)S(1)}, bf16[8,8,1,256]{3,2,1,0:T(2,128)(2,1)S(1)}, u32[]{:S(2)}, u32[]{:S(2)}) collective-permute-start(bf16[8,8,1,256]{3,2,1,0:T(2,128)(2,1)S(1)} %slice.294), channel_id=1, source_target_pairs={{1,0},{2,1},{3,2},{4,3},{5,4},{6,5},{7,6},{0,7},{9,8},{10,9},{11,1... | collective-permute-start | bytes 98312 | tf_op jit(solution)/shard_map/ppermute | solution.py:16
  17.2 2.2 collective-permute-done.1
  20.2 4.5 collective-permute-done.2
  32.4 3.1 collective-permute-done.3
  35.6 6.3 %collective-permute-done.4 = f32[8,1,17,256]{3,2,1,0:T(8,128)S(1)} collective-permute-done((f32[8,1,17,256]{3,2,1,0:T(8,128)S(1)}, f32[8,1,17,256]{3,2,1,0:T(8,128)S(1)}, u32[]{:S(2)}, u32[]{:S(2)}) %collective-permute-start.4) | collective-permute-done | bytes 139296 | tf_op jit(solution)/shard_map/ppermute | solution.py:16
  42.4 5.6 %collective-permute-done.5 = f32[8,8,1,256]{3,2,1,0:T(1,128)S(1)} collective-permute-done((f32[8,8,1,256]{3,2,1,0:T(1,128)S(1)}, f32[8,8,1,256]{3,2,1,0:T(1,128)S(1)}, u32[]{:S(2)}, u32[]{:S(2)}) %collective-permute-start.5) | collective-permute-done | bytes 65568 | tf_op jit(solution)/shard_map/ppermute | solution.py:16
  48.6 2.1 collective-permute-start.6
  50.7 2.2 collective-permute-done.6
  53.0 2.2 collective-permute-done.7
  55.3 3.0 collective-permute-start.8
  58.3 2.4 collective-permute-done.8
  62.4 4.7 %slice.323 = bf16[1,9,1,9,2,256]{5,4,3,1,2,0:T(2,128)(2,1)S(1)} slice(bf16[1,9,1,9,17,256]{5,4,3,1,2,0:T(8,128)(2,1)} %pad_maximum_fusion.7), slice={[0:1:1], [0:9:1], [0:1:1], [0:9:1], [8:17:8], [0:256:1]} | slice | bytes 165888 | tf_op jit(solution)/shard_map/slice | solution.py:26
  71.8 2.0 collective-permute-start.9
  73.9 3.2 collective-permute-done.9
  77.2 6.3 %collective-permute-done.10 = f32[8,1,17,256]{3,2,1,0:T(8,128)S(1)} collective-permute-done((f32[8,1,17,256]{3,2,1,0:T(8,128)S(1)}, f32[8,1,17,256]{3,2,1,0:T(8,128)S(1)}, u32[]{:S(2)}, u32[]{:S(2)}) %collective-permute-start.10) | collective-permute-done | bytes 139296 | tf_op jit(solution)/shard_map/ppermute | solution.py:16
  84.0 5.3 %collective-permute-done.11 = f32[8,8,1,256]{3,2,1,0:T(1,128)S(1)} collective-permute-done((f32[8,8,1,256]{3,2,1,0:T(1,128)S(1)}, f32[8,8,1,256]{3,2,1,0:T(1,128)S(1)}, u32[]{:S(2)}, u32[]{:S(2)}) %collective-permute-start.11) | collective-permute-done | bytes 65568 | tf_op jit(solution)/shard_map/ppermute | solution.py:16
  89.9 2.1 collective-permute-start.12
  92.0 2.3 collective-permute-done.12
  94.3 2.2 collective-permute-done.13
  96.6 3.7 collective-permute-start.14
  100.3 2.3 collective-permute-done.14
  104.5 4.7 %slice.346 = bf16[1,9,1,9,2,256]{5,4,3,1,2,0:T(2,128)(2,1)S(1)} slice(bf16[1,9,1,9,17,256]{5,4,3,1,2,0:T(8,128)(2,1)} %pad_maximum_fusion.8), slice={[0:1:1], [0:9:1], [0:1:1], [0:9:1], [8:17:8], [0:256:1]} | slice | bytes 165888 | tf_op jit(solution)/shard_map/slice | solution.py:26
  113.8 1.9 collective-permute-start.15
  115.9 3.2 collective-permute-done.15
  119.1 6.3 %collective-permute-done.16 = f32[8,1,17,256]{3,2,1,0:T(8,128)S(1)} collective-permute-done((f32[8,1,17,256]{3,2,1,0:T(8,128)S(1)}, f32[8,1,17,256]{3,2,1,0:T(8,128)S(1)}, u32[]{:S(2)}, u32[]{:S(2)}) %collective-permute-start.16) | collective-permute-done | bytes 139296 | tf_op jit(solution)/shard_map/ppermute | solution.py:16
  126.1 5.3 %collective-permute-done.17 = f32[8,8,1,256]{3,2,1,0:T(1,128)S(1)} collective-permute-done((f32[8,8,1,256]{3,2,1,0:T(1,128)S(1)}, f32[8,8,1,256]{3,2,1,0:T(1,128)S(1)}, u32[]{:S(2)}, u32[]{:S(2)}) %collective-permute-start.17) | collective-permute-done | bytes 65568 | tf_op jit(solution)/shard_map/ppermute | solution.py:16
  133.1 249.1 %all-reduce.6.cloned.1.call-done = f32[256,256]{0,1:T(8,128)} async-done(((f32[256,256]{0,1:T(8,128)}), f32[256,256]{0,1:T(8,128)}) %all-reduce.6.cloned.1.call-update) | async-done | bytes 262160 | tf_op jit(solution)/shard_map/psum | solution.py:131
  384.3 11.7 %cholesky.50 = f32[128,128]{1,0:T(8,128)S(1)} custom-call(f32[128,128]{1,0:T(8,128)S(1)} %cholesky.118), custom_call_target="Cholesky" | custom-call | tf_op jit(solution)/shard_map/jit(cholesky)/cholesky | solution.py:132
  396.1 9.8 %custom-call.15 = f32[1,128,128]{1,2,0:T(8,128)S(1)} custom-call(f32[1,128,128]{2,1,0:T(8,128)S(1)} %get-tuple-element.36), custom_call_target="InvertDiagBlocksLowerTriangular" | custom-call | tf_op jit(solution)/shard_map/jit(cholesky)/cholesky | solution.py:132
  406.4 11.7 %cholesky.105 = f32[128,128]{1,0:T(8,128)S(1)} custom-call(f32[128,128]{1,0:T(8,128)S(1)} %convolution_subtract_fusion.1), custom_call_target="Cholesky" | custom-call | tf_op jit(solution)/shard_map/jit(cholesky)/cholesky | solution.py:132
  420.1 4.0 while.1
  424.1 19.7 %custom-call.16 = f32[2,128,128]{1,2,0:T(8,128)S(1)} custom-call(f32[2,128,128]{2,1,0:T(8,128)S(1)} %get-tuple-element.12), custom_call_target="InvertDiagBlocksLowerTriangular" | custom-call | tf_op jit(solution)/shard_map/jit(_solve_triangular)/triangular_solve | solution.py:133
  (137 shorter events, 40.5 us)
Async XLA Ops:
  6.5 20.4 %copy-start = (bf16[729,729]{1,0:T(8,128)(2,1)S(1)}, bf16[729,729]{1,0:T(8,128)(2,1)}, u32[]{:S(2)}) copy-start(bf16[729,729]{1,0:T(8,128)(2,1)} %param.4) | copy-start | bytes 3188650
  6.5 375.7 %all-reduce.6.cloned.1.call-start = ((), (), s32[]{:S(2)}) async-start(), calls=%async_computation | async-start | bytes 524288 | tf_op jit(solution)/shard_map/psum | solution.py:131
  7.6 7.8 %collective-permute-start = (bf16[8,8,1,256]{3,2,1,0:T(2,128)(2,1)S(1)}, bf16[8,8,1,256]{3,2,1,0:T(2,128)(2,1)S(1)}, u32[]{:S(2)}, u32[]{:S(2)}) collective-permute-start(bf16[8,8,1,256]{3,2,1,0:T(2,128)(2,1)S(1)} %slice.294), channel_id=1, source_target_pairs={{1,0},{2,1},{3,2},{4,3},{5,4},{6,5},{7,6},{0,7},{9,8},{10,9},{11,1... | collective-permute-start | bytes 98312 | tf_op jit(solution)/shard_map/ppermute | solution.py:16
  15.6 3.8 collective-permute-start.1
  19.4 5.2 %collective-permute-start.2 = (bf16[1,9,17,256]{3,2,1,0:T(8,128)(2,1)S(1)}, bf16[1,9,17,256]{3,2,1,0:T(8,128)(2,1)S(1)}, u32[]{:S(2)}, u32[]{:S(2)}) collective-permute-start(bf16[1,9,17,256]{3,2,1,0:T(8,128)(2,1)S(1)} %fusion.66), channel_id=1, source_target_pairs={{64,0},{128,64},{192,128},{0,192},{65,1},{129,65},{193,129},{1,193... | collective-permute-start | bytes 235016 | tf_op jit(solution)/shard_map/ppermute | solution.py:16
  30.7 4.8 %collective-permute-start.3 = (bf16[1,9,17,256]{3,2,1,0:T(8,128)(2,1)S(1)}, bf16[1,9,17,256]{3,2,1,0:T(8,128)(2,1)S(1)}, u32[]{:S(2)}, u32[]{:S(2)}) collective-permute-start(bf16[1,9,17,256]{3,2,1,0:T(8,128)(2,1)S(1)} %fusion.70), channel_id=1, source_target_pairs={{192,0},{0,64},{64,128},{128,192},{193,1},{1,65},{65,129},{129,193... | collective-permute-start | bytes 235016 | tf_op jit(solution)/shard_map/ppermute | solution.py:16
  35.5 6.3 %collective-permute-start.4 = (f32[8,1,17,256]{3,2,1,0:T(8,128)S(1)}, f32[8,1,17,256]{3,2,1,0:T(8,128)S(1)}, u32[]{:S(2)}, u32[]{:S(2)}) collective-permute-start(f32[8,1,17,256]{3,2,1,0:T(8,128)S(1)} %pad_maximum_fusion.20), channel_id=1, source_target_pairs={{56,0},{0,8},{8,16},{16,24},{24,32},{32,40},{40,48},{48,56},{57,1}... | collective-permute-start | bytes 417800 | tf_op jit(solution)/shard_map/ppermute | solution.py:16
  42.1 6.0 %copy-start.1 = (bf16[8,8,16,256]{3,2,1,0:T(8,128)(2,1)S(1)}, bf16[8,8,16,256]{3,2,1,0:T(8,128)(2,1)}, u32[]{:S(2)}) copy-start(bf16[8,8,16,256]{3,2,1,0:T(8,128)(2,1)} %param.3) | copy-start | bytes 1572868
  42.1 6.0 %copy-start.2 = (f32[8,8,16]{2,1,0:T(8,128)S(1)}, f32[8,8,16]{2,1,0:T(8,128)}, u32[]{:S(2)}) copy-start(f32[8,8,16]{2,1,0:T(8,128)} %param.5) | copy-start | bytes 12292
  42.1 5.9 %collective-permute-start.5 = (f32[8,8,1,256]{3,2,1,0:T(1,128)S(1)}, f32[8,8,1,256]{3,2,1,0:T(1,128)S(1)}, u32[]{:S(2)}, u32[]{:S(2)}) collective-permute-start(f32[8,8,1,256]{3,2,1,0:T(1,128)S(1)} %slice.390), channel_id=1, source_target_pairs={{7,0},{0,1},{1,2},{2,3},{3,4},{4,5},{5,6},{6,7},{15,8},{8,9},{9,10... | collective-permute-start | bytes 196616 | tf_op jit(solution)/shard_map/ppermute | solution.py:16
  48.6 4.3 collective-permute-start.6
  52.9 2.2 collective-permute-start.7
  55.3 5.3 %collective-permute-start.8 = (bf16[1,9,17,256]{3,2,1,0:T(8,128)(2,1)S(1)}, bf16[1,9,17,256]{3,2,1,0:T(8,128)(2,1)S(1)}, u32[]{:S(2)}, u32[]{:S(2)}) collective-permute-start(bf16[1,9,17,256]{3,2,1,0:T(8,128)(2,1)S(1)} %slice.393), channel_id=1, source_target_pairs={{64,0},{128,64},{192,128},{0,192},{65,1},{129,65},{193,129},{1,193... | collective-permute-start | bytes 235016 | tf_op jit(solution)/shard_map/ppermute | solution.py:16
  71.8 5.3 %collective-permute-start.9 = (bf16[1,9,17,256]{3,2,1,0:T(8,128)(2,1)S(1)}, bf16[1,9,17,256]{3,2,1,0:T(8,128)(2,1)S(1)}, u32[]{:S(2)}, u32[]{:S(2)}) collective-permute-start(bf16[1,9,17,256]{3,2,1,0:T(8,128)(2,1)S(1)} %fusion.71), channel_id=1, source_target_pairs={{192,0},{0,64},{64,128},{128,192},{193,1},{1,65},{65,129},{129,193... | collective-permute-start | bytes 235016 | tf_op jit(solution)/shard_map/ppermute | solution.py:16
  77.2 6.3 %collective-permute-start.10 = (f32[8,1,17,256]{3,2,1,0:T(8,128)S(1)}, f32[8,1,17,256]{3,2,1,0:T(8,128)S(1)}, u32[]{:S(2)}, u32[]{:S(2)}) collective-permute-start(f32[8,1,17,256]{3,2,1,0:T(8,128)S(1)} %pad_maximum_fusion.19), channel_id=1, source_target_pairs={{56,0},{0,8},{8,16},{16,24},{24,32},{32,40},{40,48},{48,56},{57,1}... | collective-permute-start | bytes 417800 | tf_op jit(solution)/shard_map/ppermute | solution.py:16
  83.7 5.6 %collective-permute-start.11 = (f32[8,8,1,256]{3,2,1,0:T(1,128)S(1)}, f32[8,8,1,256]{3,2,1,0:T(1,128)S(1)}, u32[]{:S(2)}, u32[]{:S(2)}) collective-permute-start(f32[8,8,1,256]{3,2,1,0:T(1,128)S(1)} %slice.407), channel_id=1, source_target_pairs={{7,0},{0,1},{1,2},{2,3},{3,4},{4,5},{5,6},{6,7},{15,8},{8,9},{9,10... | collective-permute-start | bytes 196616 | tf_op jit(solution)/shard_map/ppermute | solution.py:16
  89.9 4.3 collective-permute-start.12
  94.2 2.2 collective-permute-start.13
  96.6 6.0 %collective-permute-start.14 = (bf16[1,9,17,256]{3,2,1,0:T(8,128)(2,1)S(1)}, bf16[1,9,17,256]{3,2,1,0:T(8,128)(2,1)S(1)}, u32[]{:S(2)}, u32[]{:S(2)}) collective-permute-start(bf16[1,9,17,256]{3,2,1,0:T(8,128)(2,1)S(1)} %slice.410), channel_id=1, source_target_pairs={{64,0},{128,64},{192,128},{0,192},{65,1},{129,65},{193,129},{1,193... | collective-permute-start | bytes 235016 | tf_op jit(solution)/shard_map/ppermute | solution.py:16
  113.8 5.2 %collective-permute-start.15 = (bf16[1,9,17,256]{3,2,1,0:T(8,128)(2,1)S(1)}, bf16[1,9,17,256]{3,2,1,0:T(8,128)(2,1)S(1)}, u32[]{:S(2)}, u32[]{:S(2)}) collective-permute-start(bf16[1,9,17,256]{3,2,1,0:T(8,128)(2,1)S(1)} %fusion.72), channel_id=1, source_target_pairs={{192,0},{0,64},{64,128},{128,192},{193,1},{1,65},{65,129},{129,193... | collective-permute-start | bytes 235016 | tf_op jit(solution)/shard_map/ppermute | solution.py:16
  119.1 6.3 %collective-permute-start.16 = (f32[8,1,17,256]{3,2,1,0:T(8,128)S(1)}, f32[8,1,17,256]{3,2,1,0:T(8,128)S(1)}, u32[]{:S(2)}, u32[]{:S(2)}) collective-permute-start(f32[8,1,17,256]{3,2,1,0:T(8,128)S(1)} %pad_maximum_fusion.18), channel_id=1, source_target_pairs={{56,0},{0,8},{8,16},{16,24},{24,32},{32,40},{40,48},{48,56},{57,1}... | collective-permute-start | bytes 417800 | tf_op jit(solution)/shard_map/ppermute | solution.py:16
  125.7 5.7 %collective-permute-start.17 = (f32[8,8,1,256]{3,2,1,0:T(1,128)S(1)}, f32[8,8,1,256]{3,2,1,0:T(1,128)S(1)}, u32[]{:S(2)}, u32[]{:S(2)}) collective-permute-start(f32[8,8,1,256]{3,2,1,0:T(1,128)S(1)} %slice.424), channel_id=1, source_target_pairs={{7,0},{0,1},{1,2},{2,3},{3,4},{4,5},{5,6},{6,7},{15,8},{8,9},{9,10... | collective-permute-start | bytes 196616 | tf_op jit(solution)/shard_map/ppermute | solution.py:16
Sparse Core Ops, SparseCore 0:
  133.1 249.0 all-reduce.5
where the time goes:
time: 462 us; the launch traced here: 453 us
  waiting for transfers between devices  315 us (68%)
  other arithmetic  67.7 us (15%)
  starting transfers between devices  25 us (5%)
  local copies, waits for them, and re-layouts  23.7 us (5%)
  between operations  15.6 us (3%)
  matrix products  6.1 us (1%)
    psum x1, waiting for transfers between devices, local(): gram = lax.psum(local_gram, ('gx', 'gy', 'gz'))  249 us
    ppermute x18, waiting for transfers between devices, passed_along(): return lax.ppermute(block, axis, route)  65.7 us
    another operation x6, other arithmetic, local(): lower = jnp.linalg.cholesky(gram / node_total)  33.9 us
    ppermute x18, starting transfers between devices, passed_along(): return lax.ppermute(block, axis, route)  25 us
    another operation x3, other arithmetic, local(): jax.scipy.linalg.solve_triangular(lower, jnp.eye(width, dtype=jnp.float32...  19.7 us
    slice x3, local copies, waits for them, and re-layouts, windows(): lax.slice_in_dim(values, POLY, span + 1, stride=POLY, axis=which_axis)  9.76 us
  transfers between devices with their start and end apart: 19, of which 19 were waited for; matrix products, arithmetic and copies ran while one was open for 0% of the time, Pallas kernels for 0%

commit v1 on v0

v1 whole, which is shorter than its diff:
```python
import functools

import jax
import jax.numpy as jnp
import ml_dtypes
import numpy as np
from jax import lax
from jax.experimental import pallas as pl
from jax.experimental.pallas import tpu as pltpu
from jax.sharding import PartitionSpec as P

POLY = 8
SIDE = POLY + 1
CENTER = 6.0
HALF_WIDTH = 8.0
MESH = pl.DeviceIdType.MESH
F32 = jnp.float32
BF16 = jnp.bfloat16

COLS = SIDE * SIDE * POLY
ROWS = 736
PLANE = ROWS - COLS
LINE = SIDE * POLY

DIRECTIONS = [
    (dx, dy, dz)
    for dx, dy, dz in [
        (-1, 0, 0), (1, 0, 0), (0, -1, 0), (0, 1, 0), (0, 0, -1), (0, 0, 1),
    ]
] + [
    (dx, dy, dz)
    for dx in (-1, 0, 1)
    for dy in (-1, 0, 1)
    for dz in (-1, 0, 1)
    if abs(dx) + abs(dy) + abs(dz) >= 2
]
LOW = [d for d in DIRECTIONS if max(d) <= 0]
HIGH = [d for d in DIRECTIONS if min(d) >= 0]


def column_rows(d):
    if d[2] != 0:
        return 0
    return 2 * LINE if 0 in d[:2] else 2 * POLY


def plane_rows(d):
    return 96 if d[:2] == (0, 0) else 16


OFFSET = {}
_at = 0
for _d in DIRECTIONS:
    OFFSET[_d] = _at
    _at += column_rows(_d) + plane_rows(_d)
MESSAGE_ROWS = _at


def message_rows(dirs):
    return sum(column_rows(d) + plane_rows(d) for d in dirs)


TOP = [d for d in DIRECTIONS if d[2] <= 0]
BOTTOM = [d for d in DIRECTIONS if d[2] > 0]


def edge_nodes(step):
    return [8] if step > 0 else [0] if step < 0 else list(range(SIDE))


def plane_nodes(d):
    return [(i, j) for i in edge_nodes(d[0]) for j in edge_nodes(d[1])]


def tables():
    order = np.zeros((ROWS, SIDE**3), np.float32)
    for i in range(SIDE):
        for j in range(SIDE):
            for k in range(POLY):
                order[i * LINE + j * POLY + k, i * 81 + j * 9 + k] = 1
            order[COLS + i * 9 + j, i * 81 + j * 9 + POLY] = 1
    pick = np.zeros((sum(plane_rows(d) for d in DIRECTIONS), ROWS), np.float32)
    at = 0
    for d in DIRECTIONS:
        for t, (i, j) in enumerate(plane_nodes(d)):
            pick[at + t, i * LINE + j * POLY if d[2] < 0 else COLS + i * 9 + j] = 1
        at += plane_rows(d)
    top = np.zeros((PLANE, sum(plane_rows(d) for d in TOP)), np.float32)
    at = 0
    for d in TOP:
        for t, (i, j) in enumerate(plane_nodes((-d[0], -d[1], 0))):
            top[i * 9 + j, at + t] = 1
        at += plane_rows(d)
    bottom = np.zeros((COLS, sum(plane_rows(d) for d in BOTTOM)), np.float32)
    at = 0
    for d in BOTTOM:
        for t, (i, j) in enumerate(plane_nodes((-d[0], -d[1], 0))):
            bottom[i * LINE + j * POLY, at + t] = 1
        at += plane_rows(d)
    insert = np.zeros((COLS, PLANE), np.float32)
    for i in range(SIDE):
        for j in range(SIDE):
            insert[i * LINE + j * POLY, i * 9 + j] = 1
    made = [order, pick, top, bottom, np.concatenate([insert, insert], 1), insert.T]
    return [m.astype(ml_dtypes.bfloat16) for m in made]


def dot(a, b):
    return jnp.dot(a, b, preferred_element_type=F32)


def filter_kernel(
    sizes,
    orbitals, cell, potential, order, pick, top, bottom, insert, extract,
    filtered, gram,
    operator, shift, sums, field0, field1, field2, send, recv, total, parts, planes, whole,
    send_sem, recv_sem, part_send_sem, part_recv_sem,
):
    nx, ny, nz = sizes
    me = (lax.axis_index("gx"), lax.axis_index("gy"), lax.axis_index("gz"))
    group = nx * ny
    mine = me[0] * ny + me[1]
    chunk = total.shape[0] // group

    def towards(d):
        return tuple(
            m if s == 0 else lax.rem(m + (s + n), n) for m, s, n in zip(me, d, sizes)
        )

    def member(t):
        other = lax.rem(mine + t, group)
        return other, (other // ny, lax.rem(other, ny), me[2])

    def above(t):
        return me[0], me[1], lax.rem(me[2] + t, nz)

    def tile(n):
        return pl.ds(pl.multiple_of(n * chunk, chunk), chunk)

    barrier = pltpu.get_barrier_semaphore()
    for d in DIRECTIONS:
        pl.semaphore_signal(barrier, inc=1, device_id=towards(d), device_id_type=MESH)

    @pl.loop(1, group)
    def _(t):
        pl.semaphore_signal(barrier, inc=1, device_id=member(t)[1], device_id_type=MESH)

    @pl.loop(1, nz)
    def _(t):
        pl.semaphore_signal(barrier, inc=1, device_id=above(t), device_id_type=MESH)

    def column_slices(d):
        for c in range(2):
            if d[1] == 0:
                yield c, (0 if d[0] < 0 else 8) * LINE, LINE
            else:
                for i in edge_nodes(d[0]):
                    yield c, i * LINE + (0 if d[1] < 0 else 8) * POLY, POLY

    def pack(number, dirs):
        source = jnp.concatenate([sums[0, :COLS], sums[1, COLS:]], axis=0).astype(BF16)
        small = dot(pick[...], source).astype(BF16)
        at = 0
        for d in DIRECTIONS:
            columns, width = column_rows(d), plane_rows(d)
            if d in dirs:
                if columns:
                    pieces = [sums[c, r : r + w] for c, r, w in column_slices(d)]
                    send[number, pl.ds(OFFSET[d], columns)] = jnp.concatenate(
                        pieces, axis=0
                    ).astype(BF16)
                send[number, pl.ds(OFFSET[d] + columns, width)] = small[at : at + width]
            at += width

    def copies(number, dirs):
        for d in dirs:
            rows = pl.ds(OFFSET[d], column_rows(d) + plane_rows(d))
            yield pltpu.make_async_remote_copy(
                src_ref=send.at[number, rows],
                dst_ref=recv.at[number, rows],
                send_sem=send_sem.at[number],
                recv_sem=recv_sem.at[number],
                device_id=towards(d),
                device_id_type=MESH,
            )

    def finish(number, dirs, semaphore):
        arrived = recv.at[number, pl.ds(0, message_rows(dirs))]
        pltpu.make_async_copy(arrived, arrived, semaphore.at[number]).wait()

    def unpack(number, dirs):
        for d in dirs:
            if column_rows(d):
                got = recv[number, pl.ds(OFFSET[d], column_rows(d))].astype(F32)
                at = 0
                for c, r, w in column_slices((-d[0], -d[1], 0)):
                    sums[c, r : r + w] += got[at : at + w]
                    at += w

        def plane_parts(wanted):
            return jnp.concatenate(
                [
                    recv[number, pl.ds(OFFSET[d] + column_rows(d), plane_rows(d))]
                    if d in dirs
                    else jnp.zeros((plane_rows(d), recv.shape[-1]), BF16)
                    for d in wanted
                ],
                axis=0,
            )

        if dirs is not HIGH:
            sums[1, COLS:] += dot(top[...], plane_parts(TOP))
        if dirs is not LOW:
            sums[0, :COLS] += dot(bottom[...], plane_parts(BOTTOM))

    def exchange(number, dirs, meanwhile=None):
        pack(number, dirs)
        for copy in copies(number, dirs):
            copy.start()
        if meanwhile is not None:
            meanwhile()
        finish(number, dirs, recv_sem)
        unpack(number, dirs)

    def hold(field, first, second, last):
        closing = dot(extract[...], second.astype(BF16))
        field[0] = jnp.concatenate([first, closing], axis=0).astype(BF16)
        field[1] = jnp.concatenate([second, last], axis=0).astype(BF16)

    def apply_operator(field):
        for c in range(2):
            values = field[c]
            image = dot(operator[...], values)
            sums[c, :COLS] = image[:COLS] + shift[c] * values.astype(F32)[:COLS]
            sums[c, COLS:] = image[COLS:]
        plane = sums[0, COLS:]
        high = plane.astype(BF16).astype(F32)
        split = jnp.concatenate([high, plane - high], axis=0).astype(BF16)
        sums[1, :COLS] += dot(insert[...], split)

    sums[...] = jnp.zeros_like(sums)
    shift[...] = jnp.zeros_like(shift)
    for i in range(POLY):
        layer = orbitals[i].astype(F32).reshape(POLY, 2, POLY, -1)
        scale = jnp.broadcast_to(
            (potential[i] - CENTER)[:, :, None], (POLY, 2 * POLY, layer.shape[-1])
        ).reshape(layer.shape)
        for c in range(2):
            sums[c, i * LINE : i * LINE + 64] = layer[:, c].reshape(64, -1)
            shift[c, i * LINE : i * LINE + 64] = scale[:, c].reshape(64, -1)

    def make_operator():
        turned = dot(order[...], cell[...]).astype(BF16)
        operator[...] = lax.dot_general(
            turned, order[...], (((1,), (1,)), ((), ())), preferred_element_type=F32
        ).astype(BF16)

    pl.semaphore_wait(barrier, len(DIRECTIONS) + group - 1 + nz - 1)
    exchange(0, LOW, make_operator)
    hold(field0, sums[0, :COLS], sums[1, :COLS], sums[1, COLS:])

    apply_operator(field0)
    exchange(1, DIRECTIONS)
    scaled = [sums[c] / HALF_WIDTH for c in range(2)]
    hold(field1, scaled[0][:COLS], scaled[1][:COLS], scaled[1][COLS:])

    apply_operator(field1)
    exchange(2, DIRECTIONS)
    scaled = [2.0 * sums[c] / HALF_WIDTH - field0[c].astype(F32) for c in range(2)]
    hold(field2, scaled[0][:COLS], scaled[1][:COLS], scaled[1][COLS:])

    apply_operator(field2)
    exchange(3, HIGH)
    for i in range(POLY):
        rows = slice(i * LINE, i * LINE + 64)
        halves = []
        for c in range(2):
            before = field1[c].astype(F32)[rows]
            now = 2.0 * sums[c, rows] / HALF_WIDTH - before
            halves.append(now.reshape(POLY, 1, POLY, -1))
        layer = jnp.concatenate(halves, axis=1).reshape(POLY, 2 * POLY, -1)
        filtered[i] = layer.astype(BF16)

    flat = filtered[...].reshape(-1, filtered.shape[-1])
    total[...] = lax.dot_general(
        flat, flat, (((0,), (0,)), ((), ())), preferred_element_type=F32
    )

    def part_copy(phase, source, target, device):
        return pltpu.make_async_remote_copy(
            src_ref=source,
            dst_ref=target,
            send_sem=part_send_sem.at[phase],
            recv_sem=part_recv_sem.at[phase],
            device_id=device,
            device_id_type=MESH,
        )

    def part_wait(buffer, count, semaphore):
        some = buffer.at[pl.ds(0, count)]
        pltpu.make_async_copy(some, some, semaphore).wait()

    @pl.loop(1, group)
    def _(t):
        other, device = member(t)
        part_copy(0, total.at[tile(other)], parts.at[mine], device).start()

    parts[mine] = total[tile(mine)]
    part_wait(parts, group - 1, part_recv_sem.at[0])
    planes[me[2]] = jnp.sum(parts[...], axis=0)

    @pl.loop(1, nz)
    def _(t):
        part_copy(1, planes.at[me[2]], planes.at[me[2]], above(t)).start()

    part_wait(planes, nz - 1, part_recv_sem.at[1])
    whole[tile(mine)] = jnp.sum(planes[...], axis=0)

    @pl.loop(1, group)
    def _(t):
        part_copy(2, whole.at[tile(mine)], whole.at[tile(mine)], member(t)[1]).start()

    part_wait(whole, (group - 1) * chunk, part_recv_sem.at[2])
    gram[...] = whole[...]

    for number, dirs in enumerate((LOW, DIRECTIONS, DIRECTIONS, HIGH)):
        finish(number, dirs, send_sem)
    part_wait(parts, group - 1, part_send_sem.at[0])
    part_wait(planes, nz - 1, part_send_sem.at[1])
    part_wait(whole, (group - 1) * chunk, part_send_sem.at[2])


def filter_and_gram(sizes, orbitals, cell_block, potential):
    width = orbitals.shape[-1]
    group = sizes[0] * sizes[1]
    made = tables()
    vmem = pl.BlockSpec(memory_space=pltpu.VMEM)
    return pl.pallas_call(
        functools.partial(filter_kernel, sizes),
        out_shape=[
            jax.ShapeDtypeStruct(orbitals.shape, BF16),
            jax.ShapeDtypeStruct((width, width), F32),
        ],
        in_specs=[vmem] * (3 + len(made)),
        out_specs=[vmem] * 2,
        scratch_shapes=[
            pltpu.VMEM((ROWS, ROWS), BF16),
            pltpu.VMEM((2, COLS, width), F32),
            pltpu.VMEM((2, ROWS, width), F32),
            pltpu.VMEM((2, ROWS, width), BF16),
            pltpu.VMEM((2, ROWS, width), BF16),
            pltpu.VMEM((2, ROWS, width), BF16),
            pltpu.VMEM((4, MESSAGE_ROWS, width), BF16),
            pltpu.VMEM((4, MESSAGE_ROWS, width), BF16),
            pltpu.VMEM((width, width), F32),
            pltpu.VMEM((group, width // group, width), F32),
            pltpu.VMEM((sizes[2], width // group, width), F32),
            pltpu.VMEM((width, width), F32),
            pltpu.SemaphoreType.DMA((4,)),
            pltpu.SemaphoreType.DMA((4,)),
            pltpu.SemaphoreType.DMA((3,)),
            pltpu.SemaphoreType.DMA((3,)),
        ],
        compiler_params=pltpu.CompilerParams(
            collective_id=0, has_side_effects=True, vmem_limit_bytes=48 * 2**20
        ),
    )(orbitals, cell_block, potential, *made)


def local(sizes, orbitals, cell_block, potential):
    filtered, gram = filter_and_gram(sizes, orbitals, cell_block, potential)
    width = filtered.shape[-1]
    flat_rows = filtered.reshape(-1, width)
    node_total = flat_rows.shape[0] * sizes[0] * sizes[1] * sizes[2]
    lower = jnp.linalg.cholesky(gram / node_total)
    inverse = jax.scipy.linalg.solve_triangular(
        lower, jnp.eye(width, dtype=F32), lower=True
    )
    right_factor = inverse.T
    factor_high = right_factor.astype(BF16)
    factor_low = (right_factor - factor_high.astype(F32)).astype(BF16)
    rotated = dot(flat_rows, factor_high) + dot(flat_rows, factor_low)
    return rotated.astype(BF16).reshape(filtered.shape)


def solution(mesh):
    sizes = tuple(mesh.shape[name] for name in ("gx", "gy", "gz"))
    placed = (P("gx", "gy", "gz", None), P(), P("gx", "gy", "gz"))
    return jax.shard_map(
        functools.partial(local, sizes),
        mesh=mesh,
        in_specs=placed,
        out_specs=P("gx", "gy", "gz", None),
        check_vma=False,
    )
```

time: 462 us -> 130 us (0.28)
  the two profiles are of different devices: /device:TPU:2 before, /device:TPU:1 now
where the time goes in v1:
time: 130 us; the launch traced here: 129 us
  Pallas kernels  57.6 us (44%)
  other arithmetic  54 us (42%)
  local copies, waits for them, and re-layouts  13.3 us (10%)
  matrix products  2.77 us (2%)
  between operations  1.34 us (1%)
    pallas_call x1, Pallas kernels, filter_and_gram(): pl.pallas_call(functools.partial(filter_kernel, sizes), out_shape=[jax.Sh...  57.6 us
    another operation x6, other arithmetic, local(): lower = jnp.linalg.cholesky(gram / node_total)  34 us
    another operation x3, other arithmetic, local(): jax.scipy.linalg.solve_triangular(lower, jnp.eye(width, dtype=F32), lower...  19.9 us
    unnamed x18, local copies, waits for them, and re-layouts  9.2 us
    another operation x6, local copies, waits for them, and re-layouts  3.74 us

profile of v1, /device:TPU:1, one launch (start us, length us, event | category | flops | bytes accessed | tf_op | source)
XLA Modules:
  0.0 129.1 jit_solution(6229365878414236399)
XLA Ops:
  0.0 0.1 triangular_solve.63
  0.1 0.0 copy-start
  0.1 1.2 copy-done
  1.4 0.0 copy-start.1
  1.4 1.3 copy-done.1
  2.6 1.2 copy-done.2
  3.8 1.0 copy-done.3
  4.8 1.0 copy-done.4
  5.8 1.0 copy-done.5
  6.8 0.9 copy-done.6
  7.7 0.9 copy-done.7
  8.6 0.8 copy-done.8
  9.3 57.6 %shard_map.91 = (bf16[8,8,16,256]{3,2,1,0:T(8,128)(2,1)S(1)}, f32[256,256]{1,0:T(8,128)S(1)}) custom-call(bf16[8,8,16,256]{3,2,1,0:T(8,128)(2,1)S(1)} %copy-done.3, bf16[729,729]{1,0:T(8,128)(2,1)S(1)} %copy-done, f32[8,8,16]{2,1,0:T(8,128)S(1)} %copy-done.8, bf16[736,729]{1,0:T(8,128)(2,1)S(1)} %copy-done.1, bf16[576,736]{1,0:T(8,128)(2,1)S(1)} %copy-done.2, ...), custom_call_target="tpu_custom_call" | custom-call | tf_op jit(solution)/shard_map/pallas_call | solution.py:338
  67.0 0.1 copy.10
  67.1 0.1 copy.11
  67.3 11.7 %cholesky.50 = f32[128,128]{1,0:T(8,128)S(1)} custom-call(f32[128,128]{1,0:T(8,128)S(1)} %cholesky.118), custom_call_target="Cholesky" | custom-call | tf_op jit(solution)/shard_map/jit(cholesky)/cholesky | solution.py:375
  79.1 9.8 %custom-call.15 = f32[1,128,128]{1,2,0:T(8,128)S(1)} custom-call(f32[1,128,128]{2,1,0:T(8,128)S(1)} %get-tuple-element.30), custom_call_target="InvertDiagBlocksLowerTriangular" | custom-call | tf_op jit(solution)/shard_map/jit(cholesky)/cholesky | solution.py:375
  88.9 0.2 constant_dynamic-update-slice_fusion.1
  89.1 0.3 convolution_subtract_fusion.1
  89.4 11.7 %cholesky.105 = f32[128,128]{1,0:T(8,128)S(1)} custom-call(f32[128,128]{1,0:T(8,128)S(1)} %convolution_subtract_fusion.1), custom_call_target="Cholesky" | custom-call | tf_op jit(solution)/shard_map/jit(cholesky)/cholesky | solution.py:375
  101.2 0.7 compare_reduce_fusion
  103.0 3.8 %while.1 = (s32[]{:T(128)}, f32[256,256]{1,0:T(8,128)S(1)}, s32[2,2]{1,0:T(2,128)S(1)}, f32[2,128,128]{2,1,0:T(8,128)S(1)}, s32[]{:T(128)}) while((s32[]{:T(128)}, f32[256,256]{1,0:T(8,128)S(1)}, s32[2,2]{1,0:T(2,128)S(1)}, f32[2,128,128]{2,1,0:T(8,128)S(1)}, s32[]{:T(128)}) %tuple.23), condition=%wide.while_cond, body=%wide.while_body.sunk | while | flops 2 | bytes 131189 | solution.py:376
  103.1 0.6 fusion.22
  103.7 1.3 bitcast_dynamic-update-slice_fusion.2
  105.0 0.6 fusion.22
  105.5 1.3 bitcast_dynamic-update-slice_fusion.2
  106.8 19.9 %custom-call.16 = f32[2,128,128]{1,2,0:T(8,128)S(1)} custom-call(f32[2,128,128]{2,1,0:T(8,128)S(1)} %get-tuple-element.16), custom_call_target="InvertDiagBlocksLowerTriangular" | custom-call | tf_op jit(solution)/shard_map/jit(_solve_triangular)/triangular_solve | solution.py:376
  126.7 0.3 fusion.5
  127.0 0.3 convolution_subtract_fusion
  127.3 0.3 fusion.8
  127.6 0.3 fusion.3
  127.9 1.1 fusion
  (19 shorter events, 0.2 us)
Async XLA Ops:
  0.1 1.3 copy-start
  1.4 1.3 copy-start.1
  2.6 1.2 copy-start.2
  3.8 1.0 copy-start.3
  4.8 1.0 copy-start.4
  5.8 1.0 copy-start.5
  6.8 0.9 copy-start.6
  7.7 0.9 copy-start.7
  8.6 0.8 copy-start.8

commit v2 on v1

--- a/solution.py
+++ b/solution.py
@@ -16,6 +16,8 @@
 MESH = pl.DeviceIdType.MESH
 F32 = jnp.float32
 BF16 = jnp.bfloat16
+HIGHEST = lax.Precision.HIGHEST
+TILE = 8
 
 COLS = SIDE * SIDE * POLY
 ROWS = 736
@@ -367,20 +369,100 @@
     )(orbitals, cell_block, potential, *made)
 
 
+def spread_lane(x, n):
+    return jnp.broadcast_to(x[:, n : n + 1], x.shape)
+
+
+def spread_row(x, n):
+    return jnp.broadcast_to(x[n : n + 1], x.shape)
+
+
+def inverse_factor(rows):
+    count = len(rows)
+    shape = rows[0].shape
+    height = lax.broadcasted_iota(jnp.int32, shape, 0)
+    lane = lax.broadcasted_iota(jnp.int32, shape, 1)
+    rows = list(rows)
+    made = [jnp.where(lane == height + TILE * g, 1.0, 0.0).astype(F32) for g in range(count)]
+    for b in range(count):
+        lead, image = rows[b], made[b]
+        columns = [spread_lane(lead, TILE * b + t) for t in range(TILE)]
+        recips, coefs, lead_rows, image_rows = [], [], [], []
+        pivots = jnp.ones(shape, F32)
+        for t in range(TILE):
+            pivot = spread_row(columns[t], t)
+            recips.append(1.0 / pivot)
+            pivots = jnp.where(height == t, pivot, pivots)
+            factor = jnp.where(height > t, columns[t] * recips[t], 0.0)
+            coefs.append({u: spread_row(columns[u], t) for u in range(t + 1, TILE)})
+            for u in range(t + 1, TILE):
+                columns[u] = columns[u] - factor * coefs[t][u]
+            lead_rows.append(spread_row(lead, t))
+            image_rows.append(spread_row(image, t))
+            lead = lead - factor * lead_rows[t]
+            image = image - factor * image_rows[t]
+        made[b] = image * lax.rsqrt(pivots)
+        for g in range(b + 1, count):
+            entries = [spread_lane(rows[g], TILE * b + t) for t in range(TILE)]
+            for t in range(TILE):
+                factor = entries[t] * recips[t]
+                for u in range(t + 1, TILE):
+                    entries[u] = entries[u] - factor * coefs[t][u]
+                rows[g] = rows[g] - factor * lead_rows[t]
+                made[g] = made[g] - factor * image_rows[t]
+    return jnp.concatenate(made, axis=0)
+
+
+def full(a, b, contract=((1,), (0,))):
+    return lax.dot_general(a, b, (contract, ((), ())), precision=HIGHEST, preferred_element_type=F32)
+
+
+NT = ((1,), (1,))
+
+
+def rotate_kernel(node_total, gram, filtered, out):
+    half = gram.shape[0] // 2
+    scaled = gram[...] / node_total
+
+    def groups(block):
+        return [block[TILE * g : TILE * (g + 1)] for g in range(half // TILE)]
+
+    first = inverse_factor(groups(scaled[:half, :half]))
+    below = full(scaled[half:, :half], first, NT)
+    second = inverse_factor(groups(scaled[half:, half:] - full(below, below, NT)))
+    corner = -full(second, full(below, first))
+    inverse = jnp.concatenate(
+        [
+            jnp.concatenate([first, jnp.zeros((half, half), F32)], axis=1),
+            jnp.concatenate([corner, second], axis=1),
+        ],
+        axis=0,
+    )
+    high = inverse.astype(BF16)
+    low = (inverse - high.astype(F32)).astype(BF16)
+    flat = filtered[...].reshape(-1, filtered.shape[-1])
+    dims = (NT, ((), ()))
+    rotated = lax.dot_general(flat, high, dims, preferred_element_type=F32) + lax.dot_general(
+        flat, low, dims, preferred_element_type=F32
+    )
+    out[...] = rotated.astype(BF16).reshape(out.shape)
+
+
+def rotate(node_total, gram, filtered):
+    vmem = pl.BlockSpec(memory_space=pltpu.VMEM)
+    return pl.pallas_call(
+        functools.partial(rotate_kernel, node_total),
+        out_shape=jax.ShapeDtypeStruct(filtered.shape, BF16),
+        in_specs=[vmem] * 2,
+        out_specs=vmem,
+        compiler_params=pltpu.CompilerParams(vmem_limit_bytes=32 * 2**20),
+    )(gram, filtered)
+
+
 def local(sizes, orbitals, cell_block, potential):
     filtered, gram = filter_and_gram(sizes, orbitals, cell_block, potential)
-    width = filtered.shape[-1]
-    flat_rows = filtered.reshape(-1, width)
-    node_total = flat_rows.shape[0] * sizes[0] * sizes[1] * sizes[2]
-    lower = jnp.linalg.cholesky(gram / node_total)
-    inverse = jax.scipy.linalg.solve_triangular(
-        lower, jnp.eye(width, dtype=F32), lower=True
-    )
-    right_factor = inverse.T
-    factor_high = right_factor.astype(BF16)
-    factor_low = (right_factor - factor_high.astype(F32)).astype(BF16)
-    rotated = dot(flat_rows, factor_high) + dot(flat_rows, factor_low)
-    return rotated.astype(BF16).reshape(filtered.shape)
+    node_total = filtered.size // filtered.shape[-1] * sizes[0] * sizes[1] * sizes[2]
+    return rotate(node_total, gram, filtered)
 
 
 def solution(mesh):

time: 130 us -> 77.6 us (0.60)
  other arithmetic: 54 us -> 0 us
  Pallas kernels: 57.6 us -> 67.9 us
  local copies, waits for them, and re-layouts: 13.3 us -> 9.2 us
  matrix products: 2.77 us -> 0 us
  between operations: 1.34 us -> 0.02 us
    another operation x9 -> x0, other arithmetic: 53.9 us -> none  [the longest x6 34 us: local(): lower = jnp.linalg.cholesky(gram / node_total)]
    pallas_call x0 -> x1, Pallas kernels: none -> 10.3 us  [rotate(): pl.pallas_call(functools.partial(rotate_kernel, node_total), out_shape=ja...]
    another operation x9 -> x0, local copies, waits for them, and re-layouts: 3.83 us -> none
    dot_general x2 -> x0, matrix products: 1.46 us -> none  [dot(): return jnp.dot(a, b, preferred_element_type=F32)]
    another operation x5 -> x0, matrix products: 1.31 us -> none  [the longest x3 0.84 us: local(): jax.scipy.linalg.solve_triangular(lower, jnp.eye(width, dtype=F32), lower...]
where the time goes in v2:
time: 77.6 us; the launch traced here: 77.2 us
  Pallas kernels  67.9 us (88%)
  local copies, waits for them, and re-layouts  9.2 us (12%)
    pallas_call x1, Pallas kernels, filter_and_gram(): pl.pallas_call(functools.partial(filter_kernel, sizes), out_shape=[jax.Sh...  57.6 us
    pallas_call x1, Pallas kernels, rotate(): pl.pallas_call(functools.partial(rotate_kernel, node_total), out_shape=ja...  10.3 us
    unnamed x18, local copies, waits for them, and re-layouts  9.2 us

profile of v2, /device:TPU:1, one launch (start us, length us, event | category | flops | bytes accessed | tf_op | source)
XLA Modules:
  0.0 77.2 jit_solution(7450941633853353542)
XLA Ops:
  0.0 0.0 copy-start
  0.0 1.3 %copy-done = bf16[729,729]{1,0:T(8,128)(2,1)S(1)} copy-done((bf16[729,729]{1,0:T(8,128)(2,1)S(1)}, bf16[729,729]{1,0:T(8,128)(2,1)}, u32[]{:S(2)}) %copy-start) | copy-done | bytes 1062906
  1.3 0.0 copy-start.1
  1.3 1.3 %copy-done.1 = bf16[736,729]{1,0:T(8,128)(2,1)S(1)} copy-done((bf16[736,729]{1,0:T(8,128)(2,1)S(1)}, bf16[736,729]{1,0:T(8,128)(2,1)}, u32[]{:S(2)}) %copy-start.1) | copy-done | bytes 1073112
  2.5 0.0 copy-start.2
  2.5 1.2 %copy-done.2 = bf16[576,736]{1,0:T(8,128)(2,1)S(1)} copy-done((bf16[576,736]{1,0:T(8,128)(2,1)S(1)}, bf16[576,736]{1,0:T(8,128)(2,1)}, u32[]{:S(2)}) %copy-start.2) | copy-done | bytes 847896
  3.7 0.0 copy-start.3
  3.7 1.0 %copy-done.3 = bf16[8,8,16,256]{3,2,1,0:T(8,128)(2,1)S(1)} copy-done((bf16[8,8,16,256]{3,2,1,0:T(8,128)(2,1)S(1)}, bf16[8,8,16,256]{3,2,1,0:T(8,128)(2,1)}, u32[]{:S(2)}) %copy-start.3) | copy-done | bytes 524312
  4.7 0.0 copy-start.4
  4.7 1.0 %copy-done.4 = bf16[648,176]{1,0:T(8,128)(2,1)S(1)} copy-done((bf16[648,176]{1,0:T(8,128)(2,1)S(1)}, bf16[648,176]{1,0:T(8,128)(2,1)}, u32[]{:S(2)}) %copy-start.4) | copy-done | bytes 228120
  5.7 0.0 copy-start.5
  5.7 1.0 %copy-done.5 = bf16[648,224]{1,0:T(8,128)(2,1)S(1)} copy-done((bf16[648,224]{1,0:T(8,128)(2,1)S(1)}, bf16[648,224]{1,0:T(8,128)(2,1)}, u32[]{:S(2)}) %copy-start.5) | copy-done | bytes 290328
  6.7 0.0 copy-start.6
  6.7 0.9 %copy-done.6 = bf16[88,648]{1,0:T(8,128)(2,1)S(1)} copy-done((bf16[88,648]{1,0:T(8,128)(2,1)S(1)}, bf16[88,648]{1,0:T(8,128)(2,1)}, u32[]{:S(2)}) %copy-start.6) | copy-done | bytes 114072
  7.6 0.0 copy-start.7
  7.6 0.9 %copy-done.7 = bf16[88,352]{1,0:T(8,128)(2,1)S(1)} copy-done((bf16[88,352]{1,0:T(8,128)(2,1)S(1)}, bf16[88,352]{1,0:T(8,128)(2,1)}, u32[]{:S(2)}) %copy-start.7) | copy-done | bytes 61976
  8.5 0.0 copy-start.8
  8.5 0.8 copy-done.8
  9.2 57.6 %shard_map.91 = (bf16[8,8,16,256]{3,2,1,0:T(8,128)(2,1)S(1)}, f32[256,256]{1,0:T(8,128)S(1)}) custom-call(bf16[8,8,16,256]{3,2,1,0:T(8,128)(2,1)S(1)} %copy-done.3, bf16[729,729]{1,0:T(8,128)(2,1)S(1)} %copy-done, f32[8,8,16]{2,1,0:T(8,128)S(1)} %copy-done.8, bf16[736,729]{1,0:T(8,128)(2,1)S(1)} %copy-done.1, bf16[576,736]{1,0:T(8,128)(2,1)S(1)} %copy-done.2, ...), custom_call_target="tpu_custom_call" | custom-call | tf_op jit(solution)/shard_map/pallas_call | solution.py:340
  66.9 10.3 %shard_map.92 = bf16[8,8,16,256]{3,2,1,0:T(8,128)(2,1)} custom-call(f32[256,256]{1,0:T(8,128)S(1)} %get-tuple-element.7.gram, bf16[8,8,16,256]{3,2,1,0:T(8,128)(2,1)S(1)} %get-tuple-element.8.filtered), custom_call_target="tpu_custom_call" | custom-call | tf_op jit(solution)/shard_map/pallas_call | solution.py:453
Async XLA Ops:
  0.0 1.3 %copy-start = (bf16[729,729]{1,0:T(8,128)(2,1)S(1)}, bf16[729,729]{1,0:T(8,128)(2,1)}, u32[]{:S(2)}) copy-start(bf16[729,729]{1,0:T(8,128)(2,1)} %cell.1) | copy-start | bytes 3188650
  1.3 1.3 %copy-start.1 = (bf16[736,729]{1,0:T(8,128)(2,1)S(1)}, bf16[736,729]{1,0:T(8,128)(2,1)}, u32[]{:S(2)}) copy-start(bf16[736,729]{1,0:T(8,128)(2,1)} %constant.12.clone.order) | copy-start | bytes 3219268
  2.5 1.2 %copy-start.2 = (bf16[576,736]{1,0:T(8,128)(2,1)S(1)}, bf16[576,736]{1,0:T(8,128)(2,1)}, u32[]{:S(2)}) copy-start(bf16[576,736]{1,0:T(8,128)(2,1)} %constant.13.clone.pick) | copy-start | bytes 2543620
  3.7 1.0 %copy-start.3 = (bf16[8,8,16,256]{3,2,1,0:T(8,128)(2,1)S(1)}, bf16[8,8,16,256]{3,2,1,0:T(8,128)(2,1)}, u32[]{:S(2)}) copy-start(bf16[8,8,16,256]{3,2,1,0:T(8,128)(2,1)} %orbitals.1) | copy-start | bytes 1572868
  4.7 1.0 %copy-start.4 = (bf16[648,176]{1,0:T(8,128)(2,1)S(1)}, bf16[648,176]{1,0:T(8,128)(2,1)}, u32[]{:S(2)}) copy-start(bf16[648,176]{1,0:T(8,128)(2,1)} %constant.16.clone.insert) | copy-start | bytes 684292
  5.7 1.0 %copy-start.5 = (bf16[648,224]{1,0:T(8,128)(2,1)S(1)}, bf16[648,224]{1,0:T(8,128)(2,1)}, u32[]{:S(2)}) copy-start(bf16[648,224]{1,0:T(8,128)(2,1)} %constant.15.clone.bottom) | copy-start | bytes 870916
  6.7 0.9 %copy-start.6 = (bf16[88,648]{1,0:T(8,128)(2,1)S(1)}, bf16[88,648]{1,0:T(8,128)(2,1)}, u32[]{:S(2)}) copy-start(bf16[88,648]{1,0:T(8,128)(2,1)} %constant.17.clone.extract) | copy-start | bytes 342148
  7.6 0.9 %copy-start.7 = (bf16[88,352]{1,0:T(8,128)(2,1)S(1)}, bf16[88,352]{1,0:T(8,128)(2,1)}, u32[]{:S(2)}) copy-start(bf16[88,352]{1,0:T(8,128)(2,1)} %constant.14.clone.top) | copy-start | bytes 185860
  8.5 0.8 copy-start.8

commit v3 on v2

--- a/solution.py
+++ b/solution.py
@@ -24,18 +24,16 @@
 PLANE = ROWS - COLS
 LINE = SIDE * POLY
 
-DIRECTIONS = [
-    (dx, dy, dz)
-    for dx, dy, dz in [
-        (-1, 0, 0), (1, 0, 0), (0, -1, 0), (0, 1, 0), (0, 0, -1), (0, 0, 1),
-    ]
-] + [
-    (dx, dy, dz)
-    for dx in (-1, 0, 1)
-    for dy in (-1, 0, 1)
-    for dz in (-1, 0, 1)
-    if abs(dx) + abs(dy) + abs(dz) >= 2
-]
+DIRECTIONS = sorted(
+    [
+        (dx, dy, dz)
+        for dx in (-1, 0, 1)
+        for dy in (-1, 0, 1)
+        for dz in (-1, 0, 1)
+        if (dx, dy, dz) != (0, 0, 0)
+    ],
+    key=lambda d: -sum(map(abs, d)),
+)
 LOW = [d for d in DIRECTIONS if max(d) <= 0]
 HIGH = [d for d in DIRECTIONS if min(d) >= 0]
 
@@ -113,11 +111,16 @@
 
 def filter_kernel(
     sizes,
-    orbitals, cell, potential, order, pick, top, bottom, insert, extract,
-    filtered, gram,
-    operator, shift, sums, field0, field1, field2, send, recv, total, parts, planes, whole,
-    send_sem, recv_sem, part_send_sem, part_recv_sem,
+    *refs,
 ):
+    operands = refs[:9]
+    filtered_out, gram_out = refs[9:11]
+    held = refs[11:20]
+    (
+        load_sem, store_sem, filtered, operator, shift, sums, field0, field1, field2, send, recv, total, parts, planes, whole,
+        send_sem, recv_sem, part_send_sem, part_recv_sem,
+    ) = refs[20:]
+    orbitals, potential, pick, cell, order, top, insert, extract, bottom = held
     nx, ny, nz = sizes
     me = (lax.axis_index("gx"), lax.axis_index("gy"), lax.axis_index("gz"))
     group = nx * ny
@@ -150,6 +153,13 @@
     @pl.loop(1, nz)
     def _(t):
         pl.semaphore_signal(barrier, inc=1, device_id=above(t), device_id_type=MESH)
+
+    loads = [
+        pltpu.make_async_copy(operand, place, load_sem.at[n])
+        for n, (operand, place) in enumerate(zip(operands, held))
+    ]
+    for load in loads:
+        load.start()
 
     def column_slices(d):
         for c in range(2):
@@ -242,6 +252,8 @@
 
     sums[...] = jnp.zeros_like(sums)
     shift[...] = jnp.zeros_like(shift)
+    loads[0].wait()
+    loads[1].wait()
     for i in range(POLY):
         layer = orbitals[i].astype(F32).reshape(POLY, 2, POLY, -1)
         scale = jnp.broadcast_to(
@@ -252,11 +264,14 @@
             shift[c, i * LINE : i * LINE + 64] = scale[:, c].reshape(64, -1)
 
     def make_operator():
+        for load in loads[3:]:
+            load.wait()
         turned = dot(order[...], cell[...]).astype(BF16)
         operator[...] = lax.dot_general(
             turned, order[...], (((1,), (1,)), ((), ())), preferred_element_type=F32
         ).astype(BF16)
 
+    loads[2].wait()
     pl.semaphore_wait(barrier, len(DIRECTIONS) + group - 1 + nz - 1)
     exchange(0, LOW, make_operator)
     hold(field0, sums[0, :COLS], sums[1, :COLS], sums[1, COLS:])
@@ -283,6 +298,8 @@
         layer = jnp.concatenate(halves, axis=1).reshape(POLY, 2 * POLY, -1)
         filtered[i] = layer.astype(BF16)
 
+    store = pltpu.make_async_copy(filtered, filtered_out, store_sem.at[0])
+    store.start()
     flat = filtered[...].reshape(-1, filtered.shape[-1])
     total[...] = lax.dot_general(
         flat, flat, (((0,), (0,)), ((), ())), preferred_element_type=F32
@@ -323,29 +340,37 @@
         part_copy(2, whole.at[tile(mine)], whole.at[tile(mine)], member(t)[1]).start()
 
     part_wait(whole, (group - 1) * chunk, part_recv_sem.at[2])
-    gram[...] = whole[...]
+    gram_store = pltpu.make_async_copy(whole, gram_out, store_sem.at[1])
+    gram_store.start()
 
     for number, dirs in enumerate((LOW, DIRECTIONS, DIRECTIONS, HIGH)):
         finish(number, dirs, send_sem)
     part_wait(parts, group - 1, part_send_sem.at[0])
     part_wait(planes, nz - 1, part_send_sem.at[1])
     part_wait(whole, (group - 1) * chunk, part_send_sem.at[2])
+    store.wait()
+    gram_store.wait()
 
 
 def filter_and_gram(sizes, orbitals, cell_block, potential):
     width = orbitals.shape[-1]
     group = sizes[0] * sizes[1]
-    made = tables()
-    vmem = pl.BlockSpec(memory_space=pltpu.VMEM)
+    order, pick, top, bottom, insert, extract = tables()
+    operands = [orbitals, potential, pick, cell_block, order, top, insert, extract, bottom]
+    hbm = pl.BlockSpec(memory_space=pltpu.MemorySpace.HBM)
     return pl.pallas_call(
         functools.partial(filter_kernel, sizes),
         out_shape=[
             jax.ShapeDtypeStruct(orbitals.shape, BF16),
             jax.ShapeDtypeStruct((width, width), F32),
         ],
-        in_specs=[vmem] * (3 + len(made)),
-        out_specs=[vmem] * 2,
-        scratch_shapes=[
+        in_specs=[hbm] * len(operands),
+        out_specs=[hbm] * 2,
+        scratch_shapes=[pltpu.VMEM(a.shape, a.dtype) for a in operands]
+        + [
+            pltpu.SemaphoreType.DMA((len(operands),)),
+            pltpu.SemaphoreType.DMA((2,)),
+            pltpu.VMEM(orbitals.shape, BF16),
             pltpu.VMEM((ROWS, ROWS), BF16),
             pltpu.VMEM((2, COLS, width), F32),
             pltpu.VMEM((2, ROWS, width), F32),
@@ -364,9 +389,9 @@
             pltpu.SemaphoreType.DMA((3,)),
         ],
         compiler_params=pltpu.CompilerParams(
-            collective_id=0, has_side_effects=True, vmem_limit_bytes=48 * 2**20
+            collective_id=0, has_side_effects=True, vmem_limit_bytes=62 * 2**20
         ),
-    )(orbitals, cell_block, potential, *made)
+    )(*operands)
 
 
 def spread_lane(x, n):
@@ -420,7 +445,12 @@
 NT = ((1,), (1,))
 
 
-def rotate_kernel(node_total, gram, filtered, out):
+def rotate_kernel(node_total, gram_in, filtered_in, out, gram, filtered, load_sem):
+    gram_load = pltpu.make_async_copy(gram_in, gram, load_sem.at[0])
+    gram_load.start()
+    load = pltpu.make_async_copy(filtered_in, filtered, load_sem.at[1])
+    load.start()
+    gram_load.wait()
     half = gram.shape[0] // 2
     scaled = gram[...] / node_total
 
@@ -440,6 +470,7 @@
     )
     high = inverse.astype(BF16)
     low = (inverse - high.astype(F32)).astype(BF16)
+    load.wait()
     flat = filtered[...].reshape(-1, filtered.shape[-1])
     dims = (NT, ((), ()))
     rotated = lax.dot_general(flat, high, dims, preferred_element_type=F32) + lax.dot_general(
@@ -449,13 +480,18 @@
 
 
 def rotate(node_total, gram, filtered):
-    vmem = pl.BlockSpec(memory_space=pltpu.VMEM)
+    hbm = pl.BlockSpec(memory_space=pltpu.MemorySpace.HBM)
     return pl.pallas_call(
         functools.partial(rotate_kernel, node_total),
         out_shape=jax.ShapeDtypeStruct(filtered.shape, BF16),
-        in_specs=[vmem] * 2,
-        out_specs=vmem,
-        compiler_params=pltpu.CompilerParams(vmem_limit_bytes=32 * 2**20),
+        in_specs=[hbm] * 2,
+        out_specs=pl.BlockSpec(memory_space=pltpu.VMEM),
+        scratch_shapes=[
+            pltpu.VMEM(gram.shape, F32),
+            pltpu.VMEM(filtered.shape, BF16),
+            pltpu.SemaphoreType.DMA((2,)),
+        ],
+        compiler_params=pltpu.CompilerParams(vmem_limit_bytes=62 * 2**20),
     )(gram, filtered)
 
 

time: 77.6 us -> 66.9 us (0.86)
  local copies, waits for them, and re-layouts: 9.2 us -> 0 us
  Pallas kernels: 67.9 us -> 66.6 us
    unnamed x18 -> x0, local copies, waits for them, and re-layouts: 9.2 us -> none
    pallas_call x1, Pallas kernels: 57.6 us -> 55.5 us  [filter_and_gram(): pl.pallas_call(functools.partial(filter_kernel, sizes), out_shape=[jax.Sh...]
    pallas_call x1, Pallas kernels: 10.3 us -> 11.2 us  [rotate(): pl.pallas_call(functools.partial(rotate_kernel, node_total), out_shape=ja...]
where the time goes in v3:
time: 66.9 us; the launch traced here: 66.8 us
  Pallas kernels  66.6 us (100%)
    pallas_call x1, Pallas kernels, filter_and_gram(): pl.pallas_call(functools.partial(filter_kernel, sizes), out_shape=[jax.Sh...  55.5 us
    pallas_call x1, Pallas kernels, rotate(): pl.pallas_call(functools.partial(rotate_kernel, node_total), out_shape=ja...  11.2 us

profile of v3, /device:TPU:1, one launch (start us, length us, event | category | flops | bytes accessed | tf_op | source)
XLA Modules:
  0.0 66.8 jit_solution(4513607417812954948)
XLA Ops:
  0.0 55.5 %shard_map.91 = (bf16[8,8,16,256]{3,2,1,0:T(8,128)(2,1)}, f32[256,256]{1,0:T(8,128)}) custom-call(bf16[8,8,16,256]{3,2,1,0:T(8,128)(2,1)} %refs_0_.1, f32[8,8,16]{2,1,0:T(8,128)} %refs_1_.1, bf16[576,736]{1,0:T(8,128)(2,1)} %constant.12.clone.refs_2_, bf16[729,729]{1,0:T(8,128)(2,1)} %refs_3_.1, bf16[736,729]{1,0:T(8,128)(2,1)} %constant.13.clone.refs_4_, ...), custom_call_target="tpu_custom_call" | custom-call | tf_op jit(solution)/shard_map/pallas_call | solution.py:361
  55.5 11.2 %shard_map.92 = bf16[8,8,16,256]{3,2,1,0:T(8,128)(2,1)} custom-call(f32[256,256]{1,0:T(8,128)} %get-tuple-element.7.gram_in, bf16[8,8,16,256]{3,2,1,0:T(8,128)(2,1)} %get-tuple-element.8.filtered_in), custom_call_target="tpu_custom_call" | custom-call | tf_op jit(solution)/shard_map/pallas_call | solution.py:484

commit v4 on v3

--- a/solution.py
+++ b/solution.py
@@ -133,8 +133,15 @@
         )
 
     def member(t):
-        other = lax.rem(mine + t, group)
-        return other, (other // ny, lax.rem(other, ny), me[2])
+        x, y = lax.rem(me[0] + t // ny, nx), lax.rem(me[1] + t % ny, ny)
+        return x * ny + y, (x, y, me[2])
+
+    def distance(t):
+        x, y = t // ny, t % ny
+        return min(x, nx - x) + min(y, ny - y) / 2
+
+    farthest_first = sorted(range(1, group), key=distance, reverse=True)
+    layers_farthest_first = sorted(range(1, nz), key=lambda t: -min(t, nz - t))
 
     def above(t):
         return me[0], me[1], lax.rem(me[2] + t, nz)
@@ -145,14 +152,6 @@
     barrier = pltpu.get_barrier_semaphore()
     for d in DIRECTIONS:
         pl.semaphore_signal(barrier, inc=1, device_id=towards(d), device_id_type=MESH)
-
-    @pl.loop(1, group)
-    def _(t):
-        pl.semaphore_signal(barrier, inc=1, device_id=member(t)[1], device_id_type=MESH)
-
-    @pl.loop(1, nz)
-    def _(t):
-        pl.semaphore_signal(barrier, inc=1, device_id=above(t), device_id_type=MESH)
 
     loads = [
         pltpu.make_async_copy(operand, place, load_sem.at[n])
@@ -251,19 +250,21 @@
         sums[1, :COLS] += dot(insert[...], split)
 
     sums[...] = jnp.zeros_like(sums)
-    shift[...] = jnp.zeros_like(shift)
     loads[0].wait()
-    loads[1].wait()
     for i in range(POLY):
         layer = orbitals[i].astype(F32).reshape(POLY, 2, POLY, -1)
-        scale = jnp.broadcast_to(
-            (potential[i] - CENTER)[:, :, None], (POLY, 2 * POLY, layer.shape[-1])
-        ).reshape(layer.shape)
         for c in range(2):
             sums[c, i * LINE : i * LINE + 64] = layer[:, c].reshape(64, -1)
-            shift[c, i * LINE : i * LINE + 64] = scale[:, c].reshape(64, -1)
 
     def make_operator():
+        loads[1].wait()
+        shift[...] = jnp.zeros_like(shift)
+        for i in range(POLY):
+            scale = jnp.broadcast_to(
+                (potential[i] - CENTER)[:, :, None], (POLY, 2 * POLY, shift.shape[-1])
+            ).reshape(POLY, 2, POLY, -1)
+            for c in range(2):
+                shift[c, i * LINE : i * LINE + 64] = scale[:, c].reshape(64, -1)
         for load in loads[3:]:
             load.wait()
         turned = dot(order[...], cell[...]).astype(BF16)
@@ -272,7 +273,7 @@
         ).astype(BF16)
 
     loads[2].wait()
-    pl.semaphore_wait(barrier, len(DIRECTIONS) + group - 1 + nz - 1)
+    pl.semaphore_wait(barrier, len(DIRECTIONS))
     exchange(0, LOW, make_operator)
     hold(field0, sums[0, :COLS], sums[1, :COLS], sums[1, COLS:])
 
@@ -319,8 +320,7 @@
         some = buffer.at[pl.ds(0, count)]
         pltpu.make_async_copy(some, some, semaphore).wait()
 
-    @pl.loop(1, group)
-    def _(t):
+    for t in farthest_first:
         other, device = member(t)
         part_copy(0, total.at[tile(other)], parts.at[mine], device).start()
 
@@ -328,15 +328,13 @@
     part_wait(parts, group - 1, part_recv_sem.at[0])
     planes[me[2]] = jnp.sum(parts[...], axis=0)
 
-    @pl.loop(1, nz)
-    def _(t):
+    for t in layers_farthest_first:
         part_copy(1, planes.at[me[2]], planes.at[me[2]], above(t)).start()
 
     part_wait(planes, nz - 1, part_recv_sem.at[1])
     whole[tile(mine)] = jnp.sum(planes[...], axis=0)
 
-    @pl.loop(1, group)
-    def _(t):
+    for t in farthest_first:
         part_copy(2, whole.at[tile(mine)], whole.at[tile(mine)], member(t)[1]).start()
 
     part_wait(whole, (group - 1) * chunk, part_recv_sem.at[2])
@@ -445,7 +443,7 @@
 NT = ((1,), (1,))
 
 
-def rotate_kernel(node_total, gram_in, filtered_in, out, gram, filtered, load_sem):
+def rotate_kernel(node_total, gram_in, filtered_in, out, gram, filtered, made, load_sem, store_sem):
     gram_load = pltpu.make_async_copy(gram_in, gram, load_sem.at[0])
     gram_load.start()
     load = pltpu.make_async_copy(filtered_in, filtered, load_sem.at[1])
@@ -457,26 +455,36 @@
     def groups(block):
         return [block[TILE * g : TILE * (g + 1)] for g in range(half // TILE)]
 
+    def rotated(values, factor):
+        high = factor.astype(BF16).astype(F32)
+        both = jnp.concatenate([high, factor - high], axis=0).astype(BF16)
+        image = lax.dot_general(values, both, (NT, ((), ())), preferred_element_type=F32)
+        return (image[:, :half] + image[:, half:]).astype(BF16)
+
     first = inverse_factor(groups(scaled[:half, :half]))
     below = full(scaled[half:, :half], first, NT)
-    second = inverse_factor(groups(scaled[half:, half:] - full(below, below, NT)))
+    rest = scaled[half:, half:] - full(below, below, NT)
+    load.wait()
+    left = filtered[..., :half].reshape(-1, half)
+    made[..., :half] = rotated(left, first).reshape(made.shape[:-1] + (half,))
+    stores = [
+        pltpu.make_async_copy(made.at[..., pl.ds(0, half)], out.at[..., pl.ds(0, half)], store_sem.at[0])
+    ]
+    stores[0].start()
+    second = inverse_factor(groups(rest))
     corner = -full(second, full(below, first))
-    inverse = jnp.concatenate(
-        [
-            jnp.concatenate([first, jnp.zeros((half, half), F32)], axis=1),
-            jnp.concatenate([corner, second], axis=1),
-        ],
-        axis=0,
-    )
-    high = inverse.astype(BF16)
-    low = (inverse - high.astype(F32)).astype(BF16)
-    load.wait()
-    flat = filtered[...].reshape(-1, filtered.shape[-1])
-    dims = (NT, ((), ()))
-    rotated = lax.dot_general(flat, high, dims, preferred_element_type=F32) + lax.dot_general(
-        flat, low, dims, preferred_element_type=F32
-    )
-    out[...] = rotated.astype(BF16).reshape(out.shape)
+    bottom = jnp.concatenate([corner, second], axis=1)
+    parts = 4
+    step = made.shape[0] // parts
+    for n in range(parts):
+        block = filtered[n * step : (n + 1) * step]
+        image = rotated(block.reshape(-1, block.shape[-1]), bottom)
+        made[n * step : (n + 1) * step, :, :, half:] = image.reshape(block.shape[:-1] + (half,))
+        where = (pl.ds(n * step, step), slice(None), slice(None), pl.ds(half, half))
+        stores.append(pltpu.make_async_copy(made.at[where], out.at[where], store_sem.at[n + 1]))
+        stores[-1].start()
+    for store in stores:
+        store.wait()
 
 
 def rotate(node_total, gram, filtered):
@@ -485,11 +493,13 @@
         functools.partial(rotate_kernel, node_total),
         out_shape=jax.ShapeDtypeStruct(filtered.shape, BF16),
         in_specs=[hbm] * 2,
-        out_specs=pl.BlockSpec(memory_space=pltpu.VMEM),
+        out_specs=hbm,
         scratch_shapes=[
             pltpu.VMEM(gram.shape, F32),
             pltpu.VMEM(filtered.shape, BF16),
+            pltpu.VMEM(filtered.shape, BF16),
             pltpu.SemaphoreType.DMA((2,)),
+            pltpu.SemaphoreType.DMA((5,)),
         ],
         compiler_params=pltpu.CompilerParams(vmem_limit_bytes=62 * 2**20),
     )(gram, filtered)

time: 66.9 us -> 64 us (0.957)
  Pallas kernels: 66.6 us -> 63.9 us
    pallas_call x1, Pallas kernels: 55.5 us -> 52.8 us  [filter_and_gram(): pl.pallas_call(functools.partial(filter_kernel, sizes), out_shape=[jax.Sh...]
where the time goes in v4:
time: 64 us; the launch traced here: 63.9 us
  Pallas kernels  63.9 us (100%)
    pallas_call x1, Pallas kernels, filter_and_gram(): pl.pallas_call(functools.partial(filter_kernel, sizes), out_shape=[jax.Sh...  52.8 us
    pallas_call x1, Pallas kernels, rotate(): pl.pallas_call(functools.partial(rotate_kernel, node_total), out_shape=ja...  11.1 us

profile of v4, /device:TPU:1, one launch (start us, length us, event | category | flops | bytes accessed | tf_op | source)
XLA Modules:
  0.0 63.9 jit_solution(4188177766983856321)
XLA Ops:
  0.0 52.8 %shard_map.91 = (bf16[8,8,16,256]{3,2,1,0:T(8,128)(2,1)}, f32[256,256]{1,0:T(8,128)}) custom-call(bf16[8,8,16,256]{3,2,1,0:T(8,128)(2,1)} %refs_0_.1, f32[8,8,16]{2,1,0:T(8,128)} %refs_1_.1, bf16[576,736]{1,0:T(8,128)(2,1)} %constant.12.clone.refs_2_, bf16[729,729]{1,0:T(8,128)(2,1)} %refs_3_.1, bf16[736,729]{1,0:T(8,128)(2,1)} %constant.13.clone.refs_4_, ...), custom_call_target="tpu_custom_call" | custom-call | tf_op jit(solution)/shard_map/pallas_call | solution.py:359
  52.8 11.1 %shard_map.92 = bf16[8,8,16,256]{3,2,1,0:T(8,128)(2,1)} custom-call(f32[256,256]{1,0:T(8,128)} %get-tuple-element.7.gram_in, bf16[8,8,16,256]{3,2,1,0:T(8,128)(2,1)} %get-tuple-element.8.filtered_in), custom_call_target="tpu_custom_call" | custom-call | tf_op jit(solution)/shard_map/pallas_call | solution.py:492

commit v5 on v4

--- a/solution.py
+++ b/solution.py
@@ -332,20 +332,20 @@
         part_copy(1, planes.at[me[2]], planes.at[me[2]], above(t)).start()
 
     part_wait(planes, nz - 1, part_recv_sem.at[1])
-    whole[tile(mine)] = jnp.sum(planes[...], axis=0)
+    whole[...] = jnp.sum(planes[...], axis=0)
+    gram_store = pltpu.make_async_copy(whole, gram_out.at[tile(mine)], store_sem.at[1])
 
     for t in farthest_first:
-        part_copy(2, whole.at[tile(mine)], whole.at[tile(mine)], member(t)[1]).start()
-
-    part_wait(whole, (group - 1) * chunk, part_recv_sem.at[2])
-    gram_store = pltpu.make_async_copy(whole, gram_out, store_sem.at[1])
+        part_copy(2, whole, gram_out.at[tile(mine)], member(t)[1]).start()
+
     gram_store.start()
+    part_wait(gram_out, (group - 1) * chunk, part_recv_sem.at[2])
 
     for number, dirs in enumerate((LOW, DIRECTIONS, DIRECTIONS, HIGH)):
         finish(number, dirs, send_sem)
     part_wait(parts, group - 1, part_send_sem.at[0])
     part_wait(planes, nz - 1, part_send_sem.at[1])
-    part_wait(whole, (group - 1) * chunk, part_send_sem.at[2])
+    part_wait(gram_out, (group - 1) * chunk, part_send_sem.at[2])
     store.wait()
     gram_store.wait()
 
@@ -380,7 +380,7 @@
             pltpu.VMEM((width, width), F32),
             pltpu.VMEM((group, width // group, width), F32),
             pltpu.VMEM((sizes[2], width // group, width), F32),
-            pltpu.VMEM((width, width), F32),
+            pltpu.VMEM((width // group, width), F32),
             pltpu.SemaphoreType.DMA((4,)),
             pltpu.SemaphoreType.DMA((4,)),
             pltpu.SemaphoreType.DMA((3,)),

time: 64 us -> 63.4 us (level)
  no operation moved by 1% of the time
where the time goes in v5:
time: 63.4 us; the launch traced here: 63.3 us
  Pallas kernels  63.3 us (100%)
    pallas_call x1, Pallas kernels, filter_and_gram(): pl.pallas_call(functools.partial(filter_kernel, sizes), out_shape=[jax.Sh...  52.2 us
    pallas_call x1, Pallas kernels, rotate(): pl.pallas_call(functools.partial(rotate_kernel, node_total), out_shape=ja...  11.1 us

profile of v5, /device:TPU:1, one launch (start us, length us, event | category | flops | bytes accessed | tf_op | source)
XLA Modules:
  0.0 63.3 jit_solution(2672822628675916502)
XLA Ops:
  0.0 52.2 %shard_map.91 = (bf16[8,8,16,256]{3,2,1,0:T(8,128)(2,1)}, f32[256,256]{1,0:T(8,128)}) custom-call(bf16[8,8,16,256]{3,2,1,0:T(8,128)(2,1)} %refs_0_.1, f32[8,8,16]{2,1,0:T(8,128)} %refs_1_.1, bf16[576,736]{1,0:T(8,128)(2,1)} %constant.12.clone.refs_2_, bf16[729,729]{1,0:T(8,128)(2,1)} %refs_3_.1, bf16[736,729]{1,0:T(8,128)(2,1)} %constant.13.clone.refs_4_, ...), custom_call_target="tpu_custom_call" | custom-call | tf_op jit(solution)/shard_map/pallas_call | solution.py:359
  52.2 11.1 %shard_map.92 = bf16[8,8,16,256]{3,2,1,0:T(8,128)(2,1)} custom-call(f32[256,256]{1,0:T(8,128)} %get-tuple-element.7.gram_in, bf16[8,8,16,256]{3,2,1,0:T(8,128)(2,1)} %get-tuple-element.8.filtered_in), custom_call_target="tpu_custom_call" | custom-call | tf_op jit(solution)/shard_map/pallas_call | solution.py:492

commit v6 on v5

--- a/solution.py
+++ b/solution.py
@@ -150,7 +150,7 @@
         return pl.ds(pl.multiple_of(n * chunk, chunk), chunk)
 
     barrier = pltpu.get_barrier_semaphore()
-    for d in DIRECTIONS:
+    for d in HIGH:
         pl.semaphore_signal(barrier, inc=1, device_id=towards(d), device_id_type=MESH)
 
     loads = [
@@ -273,7 +273,7 @@
         ).astype(BF16)
 
     loads[2].wait()
-    pl.semaphore_wait(barrier, len(DIRECTIONS))
+    pl.semaphore_wait(barrier, len(LOW))
     exchange(0, LOW, make_operator)
     hold(field0, sums[0, :COLS], sums[1, :COLS], sums[1, COLS:])
 
@@ -455,31 +455,39 @@
     def groups(block):
         return [block[TILE * g : TILE * (g + 1)] for g in range(half // TILE)]
 
-    def rotated(values, factor):
-        high = factor.astype(BF16).astype(F32)
-        both = jnp.concatenate([high, factor - high], axis=0).astype(BF16)
+    def halves(x):
+        high = x.astype(BF16)
+        return high, (x - high.astype(F32)).astype(BF16)
+
+    def product(values, factor):
+        both = jnp.concatenate(halves(factor), axis=0)
         image = lax.dot_general(values, both, (NT, ((), ())), preferred_element_type=F32)
-        return (image[:, :half] + image[:, half:]).astype(BF16)
+        return image[:, :half] + image[:, half:]
 
     first = inverse_factor(groups(scaled[:half, :half]))
     below = full(scaled[half:, :half], first, NT)
     rest = scaled[half:, half:] - full(below, below, NT)
     load.wait()
     left = filtered[..., :half].reshape(-1, half)
-    made[..., :half] = rotated(left, first).reshape(made.shape[:-1] + (half,))
+    made[..., :half] = product(left, first).astype(BF16).reshape(made.shape[:-1] + (half,))
     stores = [
         pltpu.make_async_copy(made.at[..., pl.ds(0, half)], out.at[..., pl.ds(0, half)], store_sem.at[0])
     ]
     stores[0].start()
-    second = inverse_factor(groups(rest))
-    corner = -full(second, full(below, first))
-    bottom = jnp.concatenate([corner, second], axis=1)
+    right = filtered[..., half:].reshape(-1, half).astype(F32)
+    right_high, right_low = halves(right - product(left, full(below, first)))
+    second_high, second_low = halves(inverse_factor(groups(rest)))
+    factor = jnp.concatenate([second_high, second_low, second_high], axis=1)
     parts = 4
     step = made.shape[0] // parts
+    height = left.shape[0] // parts
     for n in range(parts):
-        block = filtered[n * step : (n + 1) * step]
-        image = rotated(block.reshape(-1, block.shape[-1]), bottom)
-        made[n * step : (n + 1) * step, :, :, half:] = image.reshape(block.shape[:-1] + (half,))
+        rows = slice(n * height, (n + 1) * height)
+        values = jnp.concatenate([right_high[rows], right_high[rows], right_low[rows]], axis=1)
+        image = lax.dot_general(values, factor, (NT, ((), ())), preferred_element_type=F32)
+        made[n * step : (n + 1) * step, :, :, half:] = image.astype(BF16).reshape(
+            (step,) + made.shape[1:-1] + (half,)
+        )
         where = (pl.ds(n * step, step), slice(None), slice(None), pl.ds(half, half))
         stores.append(pltpu.make_async_copy(made.at[where], out.at[where], store_sem.at[n + 1]))
         stores[-1].start()

time: 63.4 us -> 63.1 us (level)
  no operation moved by 1% of the time
where the time goes in v6:
time: 63.1 us; the launch traced here: 63 us
  Pallas kernels  63 us (100%)
    pallas_call x1, Pallas kernels, filter_and_gram(): pl.pallas_call(functools.partial(filter_kernel, sizes), out_shape=[jax.Sh...  52.1 us
    pallas_call x1, Pallas kernels, rotate(): pl.pallas_call(functools.partial(rotate_kernel, node_total), out_shape=ja...  11 us

profile of v6, /device:TPU:1, one launch (start us, length us, event | category | flops | bytes accessed | tf_op | source)
XLA Modules:
  0.0 63.0 jit_solution(7093621573382183998)
XLA Ops:
  0.0 52.1 %shard_map.91 = (bf16[8,8,16,256]{3,2,1,0:T(8,128)(2,1)}, f32[256,256]{1,0:T(8,128)}) custom-call(bf16[8,8,16,256]{3,2,1,0:T(8,128)(2,1)} %refs_0_.1, f32[8,8,16]{2,1,0:T(8,128)} %refs_1_.1, bf16[576,736]{1,0:T(8,128)(2,1)} %constant.12.clone.refs_2_, bf16[729,729]{1,0:T(8,128)(2,1)} %refs_3_.1, bf16[736,729]{1,0:T(8,128)(2,1)} %constant.13.clone.refs_4_, ...), custom_call_target="tpu_custom_call" | custom-call | tf_op jit(solution)/shard_map/pallas_call | solution.py:359
  52.1 11.0 %shard_map.92 = bf16[8,8,16,256]{3,2,1,0:T(8,128)(2,1)} custom-call(f32[256,256]{1,0:T(8,128)} %get-tuple-element.7.gram_in, bf16[8,8,16,256]{3,2,1,0:T(8,128)(2,1)} %get-tuple-element.8.filtered_in), custom_call_target="tpu_custom_call" | custom-call | tf_op jit(solution)/shard_map/pallas_call | solution.py:500

commit v7 on v6

--- a/solution.py
+++ b/solution.py
@@ -118,7 +118,7 @@
     held = refs[11:20]
     (
         load_sem, store_sem, filtered, operator, shift, sums, field0, field1, field2, send, recv, total, parts, planes, whole,
-        send_sem, recv_sem, part_send_sem, part_recv_sem,
+        send_sem, recv_sem, plane_sem, part_send_sem, part_recv_sem,
     ) = refs[20:]
     orbitals, potential, pick, cell, order, top, insert, extract, bottom = held
     nx, ny, nz = sizes
@@ -190,7 +190,7 @@
                 src_ref=send.at[number, rows],
                 dst_ref=recv.at[number, rows],
                 send_sem=send_sem.at[number],
-                recv_sem=recv_sem.at[number],
+                recv_sem=(plane_sem if d[2] else recv_sem).at[number],
                 device_id=towards(d),
                 device_id_type=MESH,
             )
@@ -200,6 +200,7 @@
         pltpu.make_async_copy(arrived, arrived, semaphore.at[number]).wait()
 
     def unpack(number, dirs):
+        finish(number, [d for d in dirs if d[2] == 0], recv_sem)
         for d in dirs:
             if column_rows(d):
                 got = recv[number, pl.ds(OFFSET[d], column_rows(d))].astype(F32)
@@ -207,6 +208,8 @@
                 for c, r, w in column_slices((-d[0], -d[1], 0)):
                     sums[c, r : r + w] += got[at : at + w]
                     at += w
+
+        finish(number, [d for d in dirs if d[2] != 0], plane_sem)
 
         def plane_parts(wanted):
             return jnp.concatenate(
@@ -230,7 +233,6 @@
             copy.start()
         if meanwhile is not None:
             meanwhile()
-        finish(number, dirs, recv_sem)
         unpack(number, dirs)
 
     def hold(field, first, second, last):
@@ -239,7 +241,7 @@
         field[1] = jnp.concatenate([second, last], axis=0).astype(BF16)
 
     def apply_operator(field):
-        for c in range(2):
+        for c in (1, 0):
             values = field[c]
             image = dot(operator[...], values)
             sums[c, :COLS] = image[:COLS] + shift[c] * values.astype(F32)[:COLS]
@@ -381,6 +383,7 @@
             pltpu.VMEM((group, width // group, width), F32),
             pltpu.VMEM((sizes[2], width // group, width), F32),
             pltpu.VMEM((width // group, width), F32),
+            pltpu.SemaphoreType.DMA((4,)),
             pltpu.SemaphoreType.DMA((4,)),
             pltpu.SemaphoreType.DMA((4,)),
             pltpu.SemaphoreType.DMA((3,)),

time: 63.1 us -> 63.4 us (level)
  no operation moved by 1% of the time
where the time goes in v7:
time: 63.4 us; the launch traced here: 63.3 us
  Pallas kernels  63.3 us (100%)
    pallas_call x1, Pallas kernels, filter_and_gram(): pl.pallas_call(functools.partial(filter_kernel, sizes), out_shape=[jax.Sh...  52.4 us
    pallas_call x1, Pallas kernels, rotate(): pl.pallas_call(functools.partial(rotate_kernel, node_total), out_shape=ja...  11 us

profile of v7, /device:TPU:1, one launch (start us, length us, event | category | flops | bytes accessed | tf_op | source)
XLA Modules:
  0.0 63.3 jit_solution(11331837256666871173)
XLA Ops:
  0.0 52.4 %shard_map.91 = (bf16[8,8,16,256]{3,2,1,0:T(8,128)(2,1)}, f32[256,256]{1,0:T(8,128)}) custom-call(bf16[8,8,16,256]{3,2,1,0:T(8,128)(2,1)} %refs_0_.1, f32[8,8,16]{2,1,0:T(8,128)} %refs_1_.1, bf16[576,736]{1,0:T(8,128)(2,1)} %constant.12.clone.refs_2_, bf16[729,729]{1,0:T(8,128)(2,1)} %refs_3_.1, bf16[736,729]{1,0:T(8,128)(2,1)} %constant.13.clone.refs_4_, ...), custom_call_target="tpu_custom_call" | custom-call | tf_op jit(solution)/shard_map/pallas_call | solution.py:361
  52.4 11.0 %shard_map.92 = bf16[8,8,16,256]{3,2,1,0:T(8,128)(2,1)} custom-call(f32[256,256]{1,0:T(8,128)} %get-tuple-element.7.gram_in, bf16[8,8,16,256]{3,2,1,0:T(8,128)(2,1)} %get-tuple-element.8.filtered_in), custom_call_target="tpu_custom_call" | custom-call | tf_op jit(solution)/shard_map/pallas_call | solution.py:503
